TPU v7x, 32 devices: a whole 2x2x4 slice. The times are simulated.
32 devices in a mesh: dp: 4 (over z), expert: 8 (over y, x, core).
Axes of the slice: x: 2, y: 2, z: 4, core: 2. Of those that a mesh axis runs over, the one named last changes fastest.
Arguments:
- tokens: bfloat16 [1024, 7168], P('expert', 'dp'), may hold values from -6 to 6
- routes: int32 [1024, 4], P('expert'), may hold values from 0 to 7, all different within a row; in each aligned block of 128 rows (0 to 127, 128 to 255, ...) at most 96 rows name the same one
- gate_probs: float32 [1024, 4], P('expert'), may hold values from 0.05 to 0.5
- gate_up_weight: bfloat16 [8, 7168, 2, 1024], P('expert', 'dp'), may hold values from -0.0625 to 0.0625
- down_weight: bfloat16 [8, 1024, 7168], P('expert', None, 'dp'), may hold values from -0.1875 to 0.1875
- cotangent: bfloat16 [1024, 7168], P('expert', 'dp'), may hold values from -6 to 6
Outputs:
- mixed: bfloat16 [1024, 7168], P('expert', 'dp')
- token_grad: bfloat16 [1024, 7168], P('expert', 'dp')
- prob_grad: float32 [1024, 4], P('expert')
- gate_up_grad: bfloat16 [8, 7168, 2, 1024], P('expert', 'dp')
- down_grad: bfloat16 [8, 1024, 7168], P('expert', None, 'dp')
Inputs may be any that keep to these rules, and one draw needn't show every extreme that they name: `routes`: each row names 4 different experts. In each aligned block of 128 rows (the rows of one device) no expert is named by more than 96 rows, a bound that some block reaches.
All inputs are finite; a program needn't handle non-finite values.
Results may differ from a plain program's by a relative error of at most 0.0065.
Values may be sent and summed in bfloat16 or wider, within the bound.
No kernel may reach another device: no remote copies, remote signals or barrier semaphores. Data moves between devices by JAX's collectives and lax.ppermute only.
A program may use at most 128 MiB of HBM per device.

v0:
```python
import jax
import jax.numpy as jnp
from jax import lax
from jax.sharding import PartitionSpec as P


def silu_parts(pre_act):
    sigmoid_v = jax.nn.sigmoid(pre_act)
    return (pre_act * sigmoid_v, sigmoid_v * (1.0 + pre_act * (1.0 - sigmoid_v)))


def slot_table(route_block, experts, capacity):
    flat_routes = route_block.reshape(-1)
    onehot = (flat_routes[:, None] == jnp.arange(experts, dtype=jnp.int32)[None, :]).astype(
        jnp.int32
    )
    before = jnp.cumsum(onehot, axis=0) - onehot
    position = jnp.sum(before * onehot, axis=1)
    return flat_routes * capacity + position


def shards(tokens, routes, gate_probs, gate_up_weight, down_weight, cotangent):
    tok_rows, model_part = tokens.shape
    top_count = routes.shape[1]
    hidden = down_weight.shape[1]
    experts = lax.axis_size("expert")
    capacity = 3 * tok_rows * top_count // (2 * experts)
    slot_count = experts * capacity
    destination = slot_table(routes, experts, capacity)
    matches = jnp.arange(slot_count, dtype=jnp.int32)[:, None] == destination[None, :]
    picker = jnp.any(matches.reshape(slot_count, tok_rows, top_count), axis=2).astype(jnp.bfloat16)
    slot_weight = jnp.sum(jnp.where(matches, gate_probs.reshape(1, -1), 0.0), axis=1)
    token_send = jnp.dot(picker, tokens, preferred_element_type=jnp.float32).astype(jnp.bfloat16)
    token_send = token_send.reshape(experts, capacity, model_part)
    grad_send = (
        jnp.dot(picker, cotangent, preferred_element_type=jnp.float32) * slot_weight[:, None]
    ).astype(jnp.bfloat16)
    grad_send = grad_send.reshape(experts, capacity, model_part)
    joined = gate_up_weight.reshape(model_part, 2 * hidden)
    down_local = down_weight.reshape(hidden, model_part)
    token_recv = lax.all_to_all(token_send, "expert", split_axis=0, concat_axis=0, tiled=True)
    token_rows = token_recv.reshape(slot_count, model_part)
    pre_act = lax.psum(jnp.dot(token_rows, joined, preferred_element_type=jnp.float32), "dp")
    activated, slopes = silu_parts(pre_act[:, :hidden])
    hidden_act = (activated * pre_act[:, hidden:]).astype(jnp.bfloat16)
    expert_out = jnp.dot(hidden_act, down_local, preferred_element_type=jnp.float32).astype(
        jnp.bfloat16
    )
    out_send = expert_out.reshape(experts, capacity, model_part)
    out_back = lax.all_to_all(out_send, "expert", split_axis=0, concat_axis=0, tiled=True)
    grad_recv = lax.all_to_all(grad_send, "expert", split_axis=0, concat_axis=0, tiled=True)
    grad_rows = grad_recv.reshape(slot_count, model_part)
    down_grad = lax.dot_general(
        hidden_act, grad_rows, (((0,), (0,)), ((), ())), preferred_element_type=jnp.float32
    ).astype(jnp.bfloat16)
    partial_grad = lax.dot_general(
        grad_rows, down_local, (((1,), (1,)), ((), ())), preferred_element_type=jnp.float32
    )
    hidden_grad = lax.psum(partial_grad, "dp")
    act_grad = jnp.concatenate(
        [hidden_grad * pre_act[:, hidden:] * slopes, hidden_grad * activated], axis=1
    ).astype(jnp.bfloat16)
    gate_up_grad = lax.dot_general(
        token_rows, act_grad, (((0,), (0,)), ((), ())), preferred_element_type=jnp.float32
    ).astype(jnp.bfloat16)
    slot_grad = lax.dot_general(
        act_grad, joined, (((1,), (1,)), ((), ())), preferred_element_type=jnp.float32
    ).astype(jnp.bfloat16)
    grad_out_send = slot_grad.reshape(experts, capacity, model_part)
    grad_back = lax.all_to_all(grad_out_send, "expert", split_axis=0, concat_axis=0, tiled=True)
    returned = jnp.take(out_back.reshape(slot_count, model_part), destination, axis=0)
    returned = returned.reshape(tok_rows, top_count, model_part).astype(jnp.float32)
    returned_grad = jnp.take(grad_back.reshape(slot_count, model_part), destination, axis=0)
    returned_grad = returned_grad.reshape(tok_rows, top_count, model_part).astype(jnp.float32)
    mixed = jnp.sum(gate_probs[:, :, None] * returned, axis=1).astype(jnp.bfloat16)
    prob_part = jnp.sum(returned * cotangent.astype(jnp.float32)[:, None, :], axis=2)
    prob_grad = lax.psum(prob_part, "dp")
    token_grad = jnp.sum(returned_grad, axis=1).astype(jnp.bfloat16)
    return (
        mixed,
        token_grad,
        prob_grad,
        gate_up_grad.reshape(1, model_part, 2, hidden),
        down_grad.reshape(1, hidden, model_part),
    )


def solution(mesh):
    placed = (
        P("expert", "dp"),
        P("expert", None),
        P("expert", None),
        P("expert", "dp", None, None),
        P("expert", None, "dp"),
        P("expert", "dp"),
    )
    return jax.shard_map(
        shards,
        mesh=mesh,
        in_specs=placed,
        out_specs=(
            P("expert", "dp"),
            P("expert", "dp"),
            P("expert", None),
            P("expert", "dp", None, None),
            P("expert", None, "dp"),
        ),
        check_vma=False,
    )
```

profile of v0, /device:TPU:0, one launch (start us, length us, event | category | flops | bytes accessed | tf_op | source)
XLA Modules:
  0.0 578.2 jit_solution(15615102894399875981)
XLA Ops:
  7.2 0.8 copy.29
  8.3 1.1 reduce-window.6
  12.0 3.4 multiply_convert_fusion
  15.4 5.2 all-to-all-start.2
  20.6 2.4 convolution_convert_fusion.3
  23.0 31.2 %all-to-all-done.2 = bf16[8,96,1792]{2,1,0:T(8,128)(2,1)S(1)} async-done(((bf16[8,96,1792]{2,1,0:T(8,128)(2,1)}), bf16[8,96,1792]{2,1,0:T(8,128)(2,1)S(1)}, u32[]{:S(2)}, u32[]{:S(2)}) %all-to-all-start.2) | async-done | bytes 2752544 | tf_op jit(solution)/shard_map/all_to_all | solution.py:51
  54.3 4.4 all-to-all-start
  58.9 9.4 %copy.34 = bf16[224,8,2,1024]{3,1,2,0:T(8,128)(2,1)} copy(bf16[224,8,2,1024]{3,2,1,0:T(2,128)(2,1)} %bitcast.41) | data formatting | bytes 14680064
  68.3 4.7 fusion
  73.0 19.4 %all-to-all-done = bf16[8,96,1792]{2,1,0:T(8,128)(2,1)} async-done(((bf16[8,96,1792]{2,1,0:T(8,128)(2,1)}), bf16[8,96,1792]{2,1,0:T(8,128)(2,1)}, u32[]{:S(2)}, u32[]{:S(2)}) %all-to-all-start) | async-done | bytes 2752544 | tf_op jit(solution)/shard_map/all_to_all | solution.py:41
  92.4 10.6 %fusion.15 = f32[768,2048]{1,0:T(8,128)} fusion(bf16[768,1792]{1,0:T(8,128)(2,1)} %bitcast.3, bf16[1792,2048]{1,0:T(8,128)(2,1)} %bitcast.42), kind=kOutput, calls=%fused_computation.41 | convolution fusion | flops 5637144576 | bytes 16384000 | tf_op jit(solution)/shard_map/dot_general | solution.py:43
  103.0 324.9 %all-reduce.3.cloned.1.call-done = (f32[768,2048]{1,0:T(8,128)}, f32[768,1024]{1,0:T(8,128)}) async-done(((f32[768,2048]{1,0:T(8,128)}, f32[768,1024]{1,0:T(8,128)}), (f32[768,2048]{1,0:T(8,128)}, f32[768,1024]{1,0:T(8,128)})) %all-reduce.3.cloned.1.call-update) | async-done | bytes 9437200 | tf_op jit(solution)/shard_map/psum | solution.py:43
  427.9 5.7 multiply_convert_fusion.2
  433.6 11.5 %convolution_convert_fusion.2 = bf16[768,1792]{1,0:T(8,128)(2,1)} fusion(bf16[1792,2048]{1,0:T(8,128)(2,1)} %bitcast.43, bf16[768,1024]{1,0:T(8,128)(2,1)S(1)} %get-tuple-element.26, bf16[768,1024]{1,0:T(8,128)(2,1)S(1)} %get-tuple-element.25), kind=kOutput, calls=%fused_computation.12 | convolution fusion | flops 5644812288 | bytes 13238272 | tf_op jit(solution)/shard_map/dot_general | solution.py:66
  445.1 4.0 all-to-all-start.3
  449.1 2.3 mul.82
  451.4 5.2 mul.83
  456.6 7.2 %fusion.4 = bf16[768,1792]{1,0:T(8,128)(2,1)} fusion(bf16[768,1024]{1,0:T(8,128)(2,1)} %get-tuple-element.27, bf16[1,1024,1792]{2,1,0:T(8,128)(2,1)} %param.12), kind=kOutput, calls=%fused_computation.11 | convolution fusion | flops 2819948544 | bytes 7995392 | tf_op jit(solution)/shard_map/dot_general | solution.py:46
  463.7 18.8 %all-to-all-done.3 = bf16[8,96,1792]{2,1,0:T(8,128)(2,1)S(1)} async-done(((bf16[8,96,1792]{2,1,0:T(8,128)(2,1)}), bf16[8,96,1792]{2,1,0:T(8,128)(2,1)S(1)}, u32[]{:S(2)}, u32[]{:S(2)}) %all-to-all-start.3) | async-done | bytes 2752544 | tf_op jit(solution)/shard_map/all_to_all | solution.py:70
  482.6 4.4 all-to-all-start.1
  487.0 10.3 %convolution_convert_fusion = bf16[1792,2048]{1,0:T(8,128)(2,1)} fusion(bf16[768,1792]{1,0:T(8,128)(2,1)} %bitcast.3, bf16[768,1024]{1,0:T(8,128)(2,1)} %copy-done.5, bf16[768,1024]{1,0:T(8,128)(2,1)} %copy-done.4), kind=kOutput, calls=%fused_computation.2 | convolution fusion | flops 5647106048 | bytes 13238272 | tf_op jit(solution)/shard_map/dot_general | solution.py:63
  497.3 12.8 %reshape.112 = bf16[1,1792,2,1024]{3,2,1,0:T(2,128)(2,1)} reshape(bf16[1792,2048]{1,0:T(8,128)(2,1)} %convolution_convert_fusion) | data formatting | bytes 14680064 | tf_op jit(solution)/shard_map/reshape | solution.py:83
  510.1 7.2 %fusion.7 = bf16[1,1024,1792]{2,1,0:T(8,128)(2,1)} fusion(bf16[768,1024]{1,0:T(8,128)(2,1)} %get-tuple-element.27, bf16[768,1792]{1,0:T(8,128)(2,1)} %bitcast.45), kind=kOutput, calls=%fused_computation.14 | convolution fusion | flops 2820407296 | bytes 7995392 | tf_op jit(solution)/shard_map/dot_general | solution.py:53
  517.2 3.1 gather_fusion.1
  520.6 6.1 %gather_fusion = bf16[512,1792]{1,0:T(8,128)(2,1)S(1)} fusion(bf16[768,1792]{1,0:T(8,128)(2,1)} %bitcast.6, s32[1024]{0:T(1024)S(1)} %pad_clamp_fusion), kind=kCustom, calls=%fused_computation.clone | custom fusion | bytes 3672064 | tf_op jit(solution)/shard_map/jit(_take)/gather | solution.py:71
  526.7 4.4 broadcast_select_fusion
  531.1 5.1 reshape.114
  536.2 5.4 multiply_reduce_fusion.1
  541.6 4.2 reshape.111
  545.8 2.7 multiply_reduce_fusion
  548.6 17.6 %psum.23 = f32[128,4]{1,0:T(8,128)S(1)} all-reduce(f32[128,4]{1,0:T(8,128)S(1)} %reduce_sum.58), channel_id=1, replica_groups=mesh['dp'=4,'expert'=8] {'dp'}, use_global_device_ids=true, to_apply=%region_10.12 | all-reduce | flops 512 | bytes 4096 | tf_op jit(solution)/shard_map/psum | solution.py:77
  566.9 4.5 reduce_sum.56
  (36 shorter events, 4.1 us)
Async XLA Ops:
  7.2 13.4 %copy-start = (bf16[128,1792]{1,0:T(8,128)(2,1)S(1)}, bf16[128,1792]{1,0:T(8,128)(2,1)}, u32[]{:S(2)}) copy-start(bf16[128,1792]{1,0:T(8,128)(2,1)} %param.8) | copy-start | bytes 1376260
  15.4 38.8 %all-to-all-start.2 = ((bf16[8,96,1792]{2,1,0:T(8,128)(2,1)}), bf16[8,96,1792]{2,1,0:T(8,128)(2,1)S(1)}, u32[]{:S(2)}, u32[]{:S(2)}) async-start(bf16[8,96,1792]{2,1,0:T(8,128)(2,1)} %bitcast.7), calls=%async_computation.2 | async-start | bytes 5505024 | tf_op jit(solution)/shard_map/all_to_all | solution.py:51
  54.3 14.0 %copy-start.2 = (bf16[8,96,1792]{2,1,0:T(8,128)(2,1)}, bf16[8,96,1792]{2,1,0:T(8,128)(2,1)S(1)}, u32[]{:S(2)}) copy-start(bf16[8,96,1792]{2,1,0:T(8,128)(2,1)S(1)} %all-to-all-done.2) | copy-start | bytes 8257540
  54.3 38.1 %all-to-all-start = ((bf16[8,96,1792]{2,1,0:T(8,128)(2,1)}), bf16[8,96,1792]{2,1,0:T(8,128)(2,1)}, u32[]{:S(2)}, u32[]{:S(2)}) async-start(bf16[8,96,1792]{2,1,0:T(8,128)(2,1)} %bitcast.2), calls=%async_computation | async-start | bytes 5505024 | tf_op jit(solution)/shard_map/all_to_all | solution.py:41
  58.7 369.2 %all-reduce.3.cloned.1.call-start = ((), (), s32[]{:S(2)}) async-start(), calls=%async_computation.4 | async-start | bytes 18874368 | tf_op jit(solution)/shard_map/psum | solution.py:43
  58.9 9.4 %copy-start.6 = (bf16[1,1024,1792]{2,1,0:T(8,128)(2,1)S(1)}, bf16[1,1024,1792]{2,1,0:T(8,128)(2,1)}, u32[]{:S(2)}) copy-start(bf16[1,1024,1792]{2,1,0:T(8,128)(2,1)} %param.12) | copy-start | bytes 11010052
  433.6 11.5 %copy-start.4 = (bf16[768,1024]{1,0:T(8,128)(2,1)}, bf16[768,1024]{1,0:T(8,128)(2,1)S(1)}, u32[]{:S(2)}) copy-start(bf16[768,1024]{1,0:T(8,128)(2,1)S(1)} %get-tuple-element.25) | copy-start | bytes 4718596
  433.6 11.5 %copy-start.5 = (bf16[768,1024]{1,0:T(8,128)(2,1)}, bf16[768,1024]{1,0:T(8,128)(2,1)S(1)}, u32[]{:S(2)}) copy-start(bf16[768,1024]{1,0:T(8,128)(2,1)S(1)} %get-tuple-element.26) | copy-start | bytes 4718596
  445.1 4.0 copy-start.3
  445.1 37.5 %all-to-all-start.3 = ((bf16[8,96,1792]{2,1,0:T(8,128)(2,1)}), bf16[8,96,1792]{2,1,0:T(8,128)(2,1)S(1)}, u32[]{:S(2)}, u32[]{:S(2)}) async-start(bf16[8,96,1792]{2,1,0:T(8,128)(2,1)} %bitcast.47), calls=%async_computation.3 | async-start | bytes 5505024 | tf_op jit(solution)/shard_map/all_to_all | solution.py:70
  482.6 38.1 %all-to-all-start.1 = ((bf16[8,96,1792]{2,1,0:T(8,128)(2,1)}), bf16[8,96,1792]{2,1,0:T(8,128)(2,1)}, u32[]{:S(2)}, u32[]{:S(2)}) async-start(bf16[8,96,1792]{2,1,0:T(8,128)(2,1)} %bitcast.46), calls=%async_computation.1 | async-start | bytes 5505024 | tf_op jit(solution)/shard_map/all_to_all | solution.py:50
  541.6 29.7 %copy-start.1 = (bf16[128,1792]{1,0:T(8,128)(2,1)S(1)}, bf16[128,1792]{1,0:T(8,128)(2,1)}, u32[]{:S(2)}) copy-start(bf16[128,1792]{1,0:T(8,128)(2,1)} %param.8) | copy-start | bytes 1376260
Sparse Core Ops, SparseCore 0:
  103.1 324.7 all-reduce.2
where the time goes:
time: 579 us; the launch traced here: 578 us
  waiting for transfers between devices  395 us (68%)
  matrix products  57.2 us (10%)
  local copies, waits for them, and re-layouts  51.2 us (9%)
  other arithmetic  25.1 us (4%)
  starting transfers between devices  18.2 us (3%)
  blocking collectives  17.6 us (3%)
  between operations  14.2 us (2%)
    psum x1, waiting for transfers between devices, shards(): lax.psum(jnp.dot(token_rows, joined, preferred_element_type=jnp.float32),...  325 us
    all_to_all x1, waiting for transfers between devices, shards(): lax.all_to_all(grad_send, 'expert', split_axis=0, concat_axis=0, tiled=True)  31.2 us
    all_to_all x1, waiting for transfers between devices, shards(): lax.all_to_all(token_send, 'expert', split_axis=0, concat_axis=0, tiled=T...  19.4 us
    all_to_all x1, waiting for transfers between devices, shards(): lax.all_to_all(grad_out_send, 'expert', split_axis=0, concat_axis=0, tile...  18.8 us
    psum x1, blocking collectives, shards(): prob_grad = lax.psum(prob_part, 'dp')  17.6 us
    reshape x1, local copies, waits for them, and re-layouts, shards(): gate_up_grad.reshape(1, model_part, 2, hidden)  12.8 us
    unnamed x18, local copies, waits for them, and re-layouts  11.7 us
  transfers between devices with their start and end apart: 5, of which 5 were waited for; matrix products, arithmetic and copies ran while one was open for 11% of the time, Pallas kernels for 0%

commit v1 on v0

--- a/solution.py
+++ b/solution.py
@@ -2,6 +2,14 @@
 import jax.numpy as jnp
 from jax import lax
 from jax.sharding import PartitionSpec as P
+
+
+def sum_by_hops(array, name):
+    count, total = (lax.axis_size(name), array)
+    for reach in [1 << k for k in range(count.bit_length() - 1)]:
+        pairs = [(i, i ^ reach) for i in range(count)]
+        total = total + lax.ppermute(total, name, pairs)
+    return total
 
 
 def silu_parts(pre_act):
@@ -74,7 +82,7 @@
     returned_grad = returned_grad.reshape(tok_rows, top_count, model_part).astype(jnp.float32)
     mixed = jnp.sum(gate_probs[:, :, None] * returned, axis=1).astype(jnp.bfloat16)
     prob_part = jnp.sum(returned * cotangent.astype(jnp.float32)[:, None, :], axis=2)
-    prob_grad = lax.psum(prob_part, "dp")
+    prob_grad = sum_by_hops(prob_part, "dp")
     token_grad = jnp.sum(returned_grad, axis=1).astype(jnp.bfloat16)
     return (
         mixed,

time: 579 us -> 556 us (0.960)
  blocking collectives: 17.6 us -> 0 us
    all_to_all x1, waiting for transfers between devices: 18.8 us -> 0.01 us  [shards(): lax.all_to_all(grad_out_send, 'expert', split_axis=0, concat_axis=0, tile...]
    psum x1 -> x0, blocking collectives: 17.6 us -> none  [shards(): prob_grad = lax.psum(prob_part, 'dp')]
    all_to_all x1, waiting for transfers between devices: 0.27 us -> 15.2 us  [shards(): lax.all_to_all(out_send, 'expert', split_axis=0, concat_axis=0, tiled=True)]
    unnamed x18 -> x22, local copies, waits for them, and re-layouts: 11.7 us -> 11.7 us
  transfers between devices with their start and end apart: 5 -> 7, of which waited for: 5 -> 4; matrix products, arithmetic and copies ran while one was open for 11% -> 18% of each run, Pallas kernels for 0% -> 0%
where the time goes in v1:
time: 556 us; the launch traced here: 555 us
  waiting for transfers between devices  391 us (70%)
  matrix products  53.8 us (10%)
  local copies, waits for them, and re-layouts  49.6 us (9%)
  other arithmetic  26.2 us (5%)
  starting transfers between devices  20.2 us (4%)
  between operations  14.2 us (3%)
    psum x1, waiting for transfers between devices, shards(): lax.psum(jnp.dot(token_rows, joined, preferred_element_type=jnp.float32),...  325 us
    all_to_all x1, waiting for transfers between devices, shards(): lax.all_to_all(grad_send, 'expert', split_axis=0, concat_axis=0, tiled=True)  31.2 us
    all_to_all x1, waiting for transfers between devices, shards(): lax.all_to_all(token_send, 'expert', split_axis=0, concat_axis=0, tiled=T...  19.4 us
    all_to_all x1, waiting for transfers between devices, shards(): lax.all_to_all(out_send, 'expert', split_axis=0, concat_axis=0, tiled=True)  15.2 us
    reshape x1, local copies, waits for them, and re-layouts, shards(): gate_up_grad.reshape(1, model_part, 2, hidden)  12.8 us
    unnamed x22, local copies, waits for them, and re-layouts  11.7 us
  transfers between devices with their start and end apart: 7, of which 4 were waited for; matrix products, arithmetic and copies ran while one was open for 18% of the time, Pallas kernels for 0%

profile of v1, /device:TPU:0, one launch (start us, length us, event | category | flops | bytes accessed | tf_op | source)
XLA Modules:
  0.0 554.8 jit_solution(8451957400823044883)
XLA Ops:
  7.2 0.8 copy.29
  8.3 1.1 reduce-window.6
  12.0 3.4 multiply_convert_fusion
  15.4 5.2 all-to-all-start.2
  20.6 2.4 convolution_convert_fusion.3
  23.0 31.2 %all-to-all-done.2 = bf16[8,96,1792]{2,1,0:T(8,128)(2,1)S(1)} async-done(((bf16[8,96,1792]{2,1,0:T(8,128)(2,1)}), bf16[8,96,1792]{2,1,0:T(8,128)(2,1)S(1)}, u32[]{:S(2)}, u32[]{:S(2)}) %all-to-all-start.2) | async-done | bytes 2752544 | tf_op jit(solution)/shard_map/all_to_all | solution.py:59
  54.3 4.4 all-to-all-start
  58.9 9.4 %copy.34 = bf16[224,8,2,1024]{3,1,2,0:T(8,128)(2,1)} copy(bf16[224,8,2,1024]{3,2,1,0:T(2,128)(2,1)} %bitcast.41) | data formatting | bytes 14680064
  68.3 4.7 fusion
  73.0 19.4 %all-to-all-done = bf16[8,96,1792]{2,1,0:T(8,128)(2,1)} async-done(((bf16[8,96,1792]{2,1,0:T(8,128)(2,1)}), bf16[8,96,1792]{2,1,0:T(8,128)(2,1)}, u32[]{:S(2)}, u32[]{:S(2)}) %all-to-all-start) | async-done | bytes 2752544 | tf_op jit(solution)/shard_map/all_to_all | solution.py:49
  92.4 10.7 %fusion.15 = f32[768,2048]{1,0:T(8,128)} fusion(bf16[768,1792]{1,0:T(8,128)(2,1)} %bitcast.3, bf16[1792,2048]{1,0:T(8,128)(2,1)} %bitcast.42), kind=kOutput, calls=%fused_computation.41 | convolution fusion | flops 5637144576 | bytes 16384000 | tf_op jit(solution)/shard_map/dot_general | solution.py:51
  103.1 324.9 %all-reduce.3.cloned.1.call-done = (f32[768,2048]{1,0:T(8,128)}, f32[768,1024]{1,0:T(8,128)}) async-done(((f32[768,2048]{1,0:T(8,128)}, f32[768,1024]{1,0:T(8,128)}), (f32[768,2048]{1,0:T(8,128)}, f32[768,1024]{1,0:T(8,128)})) %all-reduce.3.cloned.1.call-update) | async-done | bytes 9437200 | tf_op jit(solution)/shard_map/psum | solution.py:51
  428.0 6.2 %multiply_convert_fusion.2 = (bf16[768,1024]{1,0:T(8,128)(2,1)}, bf16[768,1024]{1,0:T(8,128)(2,1)}, bf16[768,1024]{1,0:T(8,128)(2,1)S(1)}) fusion(f32[768,1024]{1,0:T(8,128)} %get-tuple-element.22, f32[768,2048]{1,0:T(8,128)} %get-tuple-element.21), kind=kLoop, calls=%fused_computation.17 | loop fusion | flops 11796480 | bytes 14155776 | tf_op jit(solution)/shard_map/convert.2
  434.2 4.4 fusion.4
  438.6 4.0 all-to-all-start.1
  442.6 2.3 mul.82
  444.9 5.2 mul.83
  450.1 10.8 %convolution_convert_fusion.2 = bf16[768,1792]{1,0:T(8,128)(2,1)} fusion(bf16[1792,2048]{1,0:T(8,128)(2,1)} %bitcast.43, bf16[768,1024]{1,0:T(8,128)(2,1)} %get-tuple-element.26, bf16[768,1024]{1,0:T(8,128)(2,1)} %get-tuple-element.25), kind=kOutput, calls=%fused_computation.12 | convolution fusion | flops 5644812288 | bytes 13238272 | tf_op jit(solution)/shard_map/dot_general | solution.py:74
  460.9 15.2 %all-to-all-done.1 = bf16[8,96,1792]{2,1,0:T(8,128)(2,1)S(1)} async-done(((bf16[8,96,1792]{2,1,0:T(8,128)(2,1)}), bf16[8,96,1792]{2,1,0:T(8,128)(2,1)S(1)}, u32[]{:S(2)}, u32[]{:S(2)}) %all-to-all-start.1) | async-done | bytes 2752544 | tf_op jit(solution)/shard_map/all_to_all | solution.py:58
  476.1 4.4 all-to-all-start.3
  480.5 10.3 %convolution_convert_fusion = bf16[1792,2048]{1,0:T(8,128)(2,1)} fusion(bf16[768,1792]{1,0:T(8,128)(2,1)} %bitcast.3, bf16[768,1024]{1,0:T(8,128)(2,1)} %get-tuple-element.26, bf16[768,1024]{1,0:T(8,128)(2,1)} %get-tuple-element.25), kind=kOutput, calls=%fused_computation.2 | convolution fusion | flops 5647106048 | bytes 13238272 | tf_op jit(solution)/shard_map/dot_general | solution.py:71
  490.8 12.8 %reshape.112 = bf16[1,1792,2,1024]{3,2,1,0:T(2,128)(2,1)} reshape(bf16[1792,2048]{1,0:T(8,128)(2,1)} %convolution_convert_fusion) | data formatting | bytes 14680064 | tf_op jit(solution)/shard_map/reshape | solution.py:91
  503.6 7.2 %fusion.7 = bf16[1,1024,1792]{2,1,0:T(8,128)(2,1)} fusion(bf16[768,1024]{1,0:T(8,128)(2,1)} %copy-done.6, bf16[768,1792]{1,0:T(8,128)(2,1)} %bitcast.45), kind=kOutput, calls=%fused_computation.14 | convolution fusion | flops 2820407296 | bytes 7995392 | tf_op jit(solution)/shard_map/dot_general | solution.py:61
  510.7 3.2 gather_fusion
  513.9 3.2 multiply_reduce_fusion
  517.4 7.1 %gather_fusion.1 = bf16[512,1792]{1,0:T(8,128)(2,1)} fusion(bf16[768,1792]{1,0:T(8,128)(2,1)} %bitcast.10, s32[1024]{0:T(1024)S(1)} %pad_clamp_fusion), kind=kCustom, calls=%fused_computation.1.clone | custom fusion | bytes 3672064 | tf_op jit(solution)/shard_map/jit(_take)/gather | solution.py:81
  524.4 4.3 broadcast_select_fusion
  528.8 5.1 reshape.114
  533.9 1.9 collective-permute-start.1
  535.8 5.5 multiply_reduce_fusion.1
  541.3 1.5 reshape.111
  542.7 4.5 reduce_sum.56
  (45 shorter events, 3.9 us)
Async XLA Ops:
  7.2 13.4 %copy-start = (bf16[128,1792]{1,0:T(8,128)(2,1)S(1)}, bf16[128,1792]{1,0:T(8,128)(2,1)}, u32[]{:S(2)}) copy-start(bf16[128,1792]{1,0:T(8,128)(2,1)} %param.8) | copy-start | bytes 1376260
  15.4 38.8 %all-to-all-start.2 = ((bf16[8,96,1792]{2,1,0:T(8,128)(2,1)}), bf16[8,96,1792]{2,1,0:T(8,128)(2,1)S(1)}, u32[]{:S(2)}, u32[]{:S(2)}) async-start(bf16[8,96,1792]{2,1,0:T(8,128)(2,1)} %bitcast.7), calls=%async_computation.2 | async-start | bytes 5505024 | tf_op jit(solution)/shard_map/all_to_all | solution.py:59
  54.3 14.0 %copy-start.4 = (bf16[8,96,1792]{2,1,0:T(8,128)(2,1)}, bf16[8,96,1792]{2,1,0:T(8,128)(2,1)S(1)}, u32[]{:S(2)}) copy-start(bf16[8,96,1792]{2,1,0:T(8,128)(2,1)S(1)} %all-to-all-done.2) | copy-start | bytes 8257540
  54.3 38.1 %all-to-all-start = ((bf16[8,96,1792]{2,1,0:T(8,128)(2,1)}), bf16[8,96,1792]{2,1,0:T(8,128)(2,1)}, u32[]{:S(2)}, u32[]{:S(2)}) async-start(bf16[8,96,1792]{2,1,0:T(8,128)(2,1)} %bitcast.2), calls=%async_computation | async-start | bytes 5505024 | tf_op jit(solution)/shard_map/all_to_all | solution.py:49
  58.7 369.3 %all-reduce.3.cloned.1.call-start = ((), (), s32[]{:S(2)}) async-start(), calls=%async_computation.4 | async-start | bytes 18874368 | tf_op jit(solution)/shard_map/psum | solution.py:51
  58.9 9.4 %copy-start.7 = (bf16[1,1024,1792]{2,1,0:T(8,128)(2,1)S(1)}, bf16[1,1024,1792]{2,1,0:T(8,128)(2,1)}, u32[]{:S(2)}) copy-start(bf16[1,1024,1792]{2,1,0:T(8,128)(2,1)} %param.12) | copy-start | bytes 11010052
  428.0 6.2 %copy-start.8 = (bf16[1,1024,1792]{2,1,0:T(8,128)(2,1)S(1)}, bf16[1,1024,1792]{2,1,0:T(8,128)(2,1)}, u32[]{:S(2)}) copy-start(bf16[1,1024,1792]{2,1,0:T(8,128)(2,1)} %param.12) | copy-start | bytes 11010052
  434.2 4.4 copy-start.6
  438.6 4.0 copy-start.5
  438.6 37.5 %all-to-all-start.1 = ((bf16[8,96,1792]{2,1,0:T(8,128)(2,1)}), bf16[8,96,1792]{2,1,0:T(8,128)(2,1)S(1)}, u32[]{:S(2)}, u32[]{:S(2)}) async-start(bf16[8,96,1792]{2,1,0:T(8,128)(2,1)} %bitcast.47), calls=%async_computation.1 | async-start | bytes 5505024 | tf_op jit(solution)/shard_map/all_to_all | solution.py:58
  476.1 41.2 %all-to-all-start.3 = ((bf16[8,96,1792]{2,1,0:T(8,128)(2,1)}), bf16[8,96,1792]{2,1,0:T(8,128)(2,1)}, u32[]{:S(2)}, u32[]{:S(2)}) async-start(bf16[8,96,1792]{2,1,0:T(8,128)(2,1)} %bitcast.46), calls=%async_computation.3 | async-start | bytes 5505024 | tf_op jit(solution)/shard_map/all_to_all | solution.py:78
  517.3 16.6 %collective-permute-start = (f32[128,4]{1,0:T(8,128)S(1)}, f32[128,4]{1,0:T(8,128)S(1)}, u32[]{:S(2)}, u32[]{:S(2)}) collective-permute-start(f32[128,4]{1,0:T(8,128)S(1)} %reduce_sum.58), channel_id=1, source_target_pairs={{0,8},{8,0},{16,24},{24,16},{1,9},{9,1},{17,25},{25,17},{2,10},{10... | collective-permute-start | bytes 6152 | tf_op jit(solution)/shard_map/ppermute | solution.py:11
  517.3 7.1 %copy-start.2 = (bf16[512,1792]{1,0:T(8,128)(2,1)S(1)}, bf16[512,1792]{1,0:T(8,128)(2,1)}, u32[]{:S(2)}) copy-start(bf16[512,1792]{1,0:T(8,128)(2,1)} %gather_fusion) | copy-start | bytes 5505028
  533.9 7.4 %copy-start.3 = (bf16[512,1792]{1,0:T(8,128)(2,1)S(1)}, bf16[512,1792]{1,0:T(8,128)(2,1)}, u32[]{:S(2)}) copy-start(bf16[512,1792]{1,0:T(8,128)(2,1)} %get-tuple-element.28) | copy-start | bytes 5505028
  533.9 13.3 %collective-permute-start.1 = (f32[128,4]{1,0:T(8,128)S(1)}, f32[128,4]{1,0:T(8,128)S(1)}, u32[]{:S(2)}, u32[]{:S(2)}) collective-permute-start(f32[128,4]{1,0:T(8,128)S(1)} %add.36), channel_id=1, source_target_pairs={{0,16},{8,24},{16,0},{24,8},{1,17},{9,25},{17,1},{25,9},{2,18},{10... | collective-permute-start | bytes 6152 | tf_op jit(solution)/shard_map/ppermute | solution.py:11
  535.8 12.1 %copy-start.1 = (bf16[128,1792]{1,0:T(8,128)(2,1)S(1)}, bf16[128,1792]{1,0:T(8,128)(2,1)}, u32[]{:S(2)}) copy-start(bf16[128,1792]{1,0:T(8,128)(2,1)} %param.8) | copy-start | bytes 1376260
Sparse Core Ops, SparseCore 0:
  103.2 324.7 all-reduce.2
